TPU v7x, 512 devices: a whole 4x8x8 slice. The times are simulated.
512 devices in a mesh: replica: 32 (over x, z), expert: 16 (over y, core).
Axes of the slice: x: 4, y: 8, z: 8, core: 2. Of those that a mesh axis runs over, the one named last changes fastest.
Arguments:
- weights: bfloat16 [32, 3, 3072, 2048], P('replica', None, 'expert'), may hold values from -0.125 to 0.125
- tokens: bfloat16 [32, 2048, 2048], P('replica', 'expert'), may hold values from -6 to 6
- cotangent: bfloat16 [32, 2048, 2048], P('replica', 'expert'), may hold values from -6 to 6
- routes: int32 [32, 2048, 1], P('replica', 'expert'), may hold values from 0 to 3; in each aligned block of 128 rows (0 to 127, 128 to 255, ..., all dimensions but the last counted through in order) at most 44 rows name the same one
- gate_weights: float32 [32, 2048, 1], P('replica', 'expert'), may hold values from 0.25 to 1
- next_tokens: bfloat16 [32, 2048, 2048], P('replica', 'expert'), may hold values from -6 to 6
- next_routes: int32 [32, 2048, 1], P('replica', 'expert'), may hold values from 0 to 3; in each aligned block of 128 rows (0 to 127, 128 to 255, ..., all dimensions but the last counted through in order) at most 44 rows name the same one
- next_gates: float32 [32, 2048, 1], P('replica', 'expert'), may hold values from 0.25 to 1
- step_index: int32 [1], replicated, may hold values from 0 to 63
Outputs:
- token_codes: bfloat16 [32, 2048, 2048], P('replica', 'expert')
- token_scales: float32 [32, 2048], P('replica', 'expert')
Inputs may be any that keep to these rules, and one draw needn't show every extreme that they name: `routes`: in the 128 tokens of one device, no expert is named more than 44 times, a bound that some block reaches; a token names 1 different experts. `next_routes`: in the 128 tokens of one device, no expert is named more than 44 times, a bound that some block reaches; a token names 1 different experts.
All inputs are finite; a program needn't handle non-finite values. Where the computation divides by a largest or mean magnitude, that divisor is 1e-20 or more.
Results may differ from a plain program's by a relative error of at most 0.025.
Values may be sent and summed in bfloat16 or wider, within the bound.
A program may use at most 128 MiB of HBM per device.

v0:
```python
import functools
import math

import jax
import jax.numpy as jnp
from jax import lax
from jax.experimental import pallas as pl
from jax.experimental.pallas import tpu as pltpu
from jax.sharding import PartitionSpec as P

D = 2048
EXPERTS = 4
CAP = 44
ROWS = 48
TOK = 128
HID = 192
CHIPS = 8
LEVELS = 4
COLS = 512
CHUNKS = D // COLS
GROUP = 4 * ROWS
KINDS = 3
EARLY = (3, 2, 2, 3)
RATE = 2.0 / math.sqrt(D * 16 * CAP)
epsilon = 1e-06
MESH = pl.DeviceIdType.MESH
contract_last = (((1,), (1,)), ((), ()))
contract_rows = (((0,), (0,)), ((), ()))


def dot(a, b):
    return jnp.dot(a, b, preferred_element_type=jnp.float32)


def dot_last(a, b):
    return lax.dot_general(a, b, contract_last, preferred_element_type=jnp.float32)


def column(row):
    lane = lax.broadcasted_iota(jnp.int32, (TOK, TOK), 1)
    across = lax.broadcasted_iota(jnp.int32, (TOK, TOK), 0)
    return jnp.sum(jnp.where(lane == across, row, 0.0), axis=1, keepdims=True)


def one_hot_of(routes):
    lane = lax.broadcasted_iota(jnp.int32, (TOK, TOK), 1)
    across = lax.broadcasted_iota(jnp.int32, (TOK, TOK), 0)
    earlier = (across < lane).astype(jnp.bfloat16)
    named = lax.broadcasted_iota(jnp.int32, (16, TOK), 0) == routes
    before = dot(named.astype(jnp.bfloat16), earlier)
    slot = jnp.sum(jnp.where(named, before, 0.0), axis=0, keepdims=True)
    target = routes * ROWS + slot.astype(jnp.int32)
    place = lax.broadcasted_iota(jnp.int32, (EXPERTS * ROWS, TOK), 0)
    return (place == target).astype(jnp.float32)


def columns(c):
    return pl.ds(pl.multiple_of(c * COLS, COLS), COLS)


def kernel(
    level,
    routes_ref,
    gates_ref,
    next_routes_ref,
    next_gates_ref,
    tok_hbm,
    cot_hbm,
    nxt_hbm,
    w_hbm,
    codes_ref,
    scales_ref,
    held,
    w_ref,
    block,
    rows,
    gate_t,
    up_t,
    back_t,
    d_t,
    own,
    theirs,
    acc,
    hid,
    hid_in,
    down,
    out,
    ret,
    mixed,
    table,
    l_sem,
    x_send,
    x_recv,
    g_send,
    g_recv,
    h_send,
    h_recv,
    d_send,
    d_recv,
    o_send,
    o_recv,
):
    r = lax.axis_index("replica")
    e = lax.axis_index("expert")
    y = lax.div(e, 2)
    k = lax.rem(e, 2)
    side = 2 * lax.rem(y, 2) - 1
    mine = lax.div(y, 2)

    def chip(hops):
        return lax.rem(y + side * hops + 2 * CHIPS, CHIPS)

    def same_core(hops):
        return (r, chip(hops) * 2 + k)

    def other_core(hops):
        return (r, chip(hops) * 2 + 1 - k)

    def expert_at(hops):
        return lax.div(chip(hops), 2)

    apart = 1 << level
    partner = (r + apart * (1 - 2 * lax.rem(lax.div(r, apart), 2)), e)

    def remote(src, dst, send, recv, to):
        return pltpu.make_async_remote_copy(
            src_ref=src, dst_ref=dst, send_sem=send, recv_sem=recv, device_id=to, device_id_type=MESH
        )

    barrier = pltpu.get_barrier_semaphore()
    peers = [same_core(h) for h in (1, 2, 3, -1, -2)] + [other_core(0), other_core(-1), partner]
    for peer in peers:
        pl.semaphore_signal(barrier, inc=1, device_id=peer, device_id_type=MESH)
    def over(first, last, body):
        def run(p, carry):
            body(p)
            return carry

        lax.fori_loop(first, last, run, 0)

    def load_tokens(c):
        return pltpu.make_async_copy(tok_hbm.at[:, columns(c)], held.at[0, :, columns(c)], l_sem.at[c])

    over(0, CHUNKS, lambda c: load_tokens(c).start())
    loads = [
        pltpu.make_async_copy(src, dst, l_sem.at[CHUNKS + n])
        for n, (src, dst) in enumerate(((cot_hbm, held.at[1]), (nxt_hbm, held.at[2]), (w_hbm, w_ref)))
    ]
    for load in loads:
        load.start()
    early_chunks = EARLY[level]

    def place(p, lane, slot):
        return rows.at[p, lane * 2 + slot // 4, slot % 4]

    def direct(p):
        copies = [
            remote(
                block.at[p, expert_at(hops)], place(p, 0, slot), x_send.at[p, n], x_recv.at[p, slot], same_core(hops)
            )
            for n, (slot, hops) in enumerate(((1, 1), (3, 3), (2, -2), (4, -1)))
        ]
        return copies + [
            remote(block.at[p, mine], place(p, 1, 0), x_send.at[p, 4], x_recv.at[p, 8], other_core(0))
        ]

    def relay(p, slot):
        return remote(
            place(p, 0, slot), place(p, 0, slot + 4), x_send.at[p, 11 + slot], x_recv.at[p, slot + 4], same_core(-1)
        )

    def forward(p, slot):
        return remote(
            place(p, 0, slot), place(p, 1, slot), x_send.at[p, 4 + slot], x_recv.at[p, 8 + slot], other_core(0)
        )

    def dispatch(p):
        for copy in direct(p):
            copy.start()
        rows[p, 0, 0] = block[p, mine]

    def takes(p, slots):
        for slot in slots:
            remote(
                place(p, 0, slot), place(p, 0, slot), x_send.at[p, 0], x_recv.at[p, slot], other_core(0)
            ).wait_recv()
            if slot < 4:
                relay(p, slot).start()
            forward(p, slot).start()

    def take_lane(p, slots):
        for slot in slots:
            remote(
                place(p, 1, slot), place(p, 1, slot), x_send.at[p, 0], x_recv.at[p, 8 + slot], other_core(0)
            ).wait_recv()

    def place_rows(p, hot, scale):
        value = held[p // CHUNKS, :, columns(p % CHUNKS)]
        if scale is not None:
            value = (scale * value.astype(jnp.float32)).astype(jnp.bfloat16)
        block[p] = dot(hot, value).astype(jnp.bfloat16).reshape(EXPERTS, ROWS, COLS)

    hot = one_hot_of(routes_ref[...]).astype(jnp.bfloat16)
    load_tokens(0).wait()
    place_rows(0, hot, None)
    pl.semaphore_wait(barrier, len(peers))
    dispatch(0)

    def place_x(p):
        load_tokens(p).wait()
        place_rows(p, hot, None)
        dispatch(p)

    over(1, 4, place_x)
    loads[0].wait()
    gates = column(gates_ref[...])
    over(4, 8, lambda p: place_rows(p, hot, gates))
    dispatch(4)
    hot_next = one_hot_of(next_routes_ref[...])
    hot_next_rows = hot_next.astype(jnp.bfloat16)
    loads[1].wait()
    over(8, 12, lambda p: place_rows(p, hot_next_rows, None))
    table[...] = hot_next.T.astype(jnp.bfloat16)
    loads[2].wait()

    def group(kind, q, c):
        return rows[kind * CHUNKS + c, q].reshape(GROUP, COLS)

    def forward_x(q):
        gate_t[q] = jnp.zeros((HID, GROUP), jnp.float32)
        up_t[q] = jnp.zeros((HID, GROUP), jnp.float32)
        back_t[q] = jnp.zeros((HID, GROUP), jnp.float32)

        def body(c):
            value = group(0, q, c)
            gate_t[q] += dot_last(w_ref[0, :, columns(c)], value)
            up_t[q] += dot_last(w_ref[1, :, columns(c)], value)

        over(0, CHUNKS, body)
        gate = gate_t[q]
        d_t[2, q] = (gate * jax.nn.sigmoid(gate) * up_t[q]).astype(jnp.bfloat16)

    def backward(q, c):
        back_t[q] += dot_last(w_ref[2, :, columns(c)], group(1, q, c))

    def slopes(q):
        back = back_t[q]
        gate = gate_t[q]
        up = up_t[q]
        logistic = jax.nn.sigmoid(gate)
        d_t[0, q] = (back * up * (logistic * (1.0 + gate * (1.0 - logistic)))).astype(jnp.bfloat16)
        d_t[1, q] = (back * (gate * logistic)).astype(jnp.bfloat16)

    def exchange(index):
        return remote(own.at[index], theirs.at[index], g_send.at[index], g_recv.at[index], partner)

    def update(j, c, index):
        cols = columns(c)
        kind = j // 2
        grad = jnp.zeros((HID, COLS), jnp.float32)
        for q in range(4):
            grad += dot(d_t[j, q], group(kind, q, c))
        grad = grad.astype(jnp.bfloat16).astype(jnp.float32)
        own[index] = (w_ref[j, :, cols].astype(jnp.float32) - RATE * grad).astype(jnp.bfloat16)
        exchange(index).start()

    def update_up(c):
        over(0, 2, lambda j: update(j, c, 2 * c + j))
        takes(8 + c, near)

    def update_down(c):
        update(2, c, 2 * CHUNKS + c)

    near, rest = (1, 2, 3), (4, 5, 6, 7)
    over(0, 4, lambda p: takes(p, near))
    dispatch(5)

    def forward_half(half):
        @pl.when(half == 1)
        def _():
            over(0, 4, lambda p: takes(p, rest))

        over(0, 4, lambda p: take_lane(p, [4 * half + n for n in range(4)]))
        over(0, 2, lambda lane: forward_x(2 * lane + half))
        takes(4 + half, near)
        dispatch(6 + half)

    over(0, 2, forward_half)

    def early(c):
        takes(c + 4, rest)
        take_lane(c + 4, range(8))

        @pl.when(c < early_chunks)
        def _():
            update_down(c)

        over(0, 4, lambda q: backward(q, c))

        @pl.when(c < 2)
        def _():
            takes(c + 6, near)

    over(0, 3, early)
    takes(7, rest)
    over(8, 12, dispatch)
    take_lane(7, range(8))

    def backward_last(q):
        backward(q, CHUNKS - 1)
        slopes(q)

    over(0, 4, backward_last)
    over(0, CHUNKS, update_up)
    over(early_chunks, CHUNKS, update_down)

    def averaged(index):
        exchange(index).wait_recv()
        both = own[index].astype(jnp.float32) + theirs[index].astype(jnp.float32)
        return (both * 0.5).astype(jnp.bfloat16)

    def to_core(c):
        return remote(down.at[0, c], down.at[1, c], d_send.at[0, c], d_recv.at[0, c], other_core(0))

    def to_pair(c):
        return remote(down.at[0, c], down.at[2, c], d_send.at[1, c], d_recv.at[1, c], same_core(-1))

    def pair_to_core(c):
        return remote(down.at[2, c], down.at[3, c], d_send.at[2, c], d_recv.at[2, c], other_core(0))

    def give_back(c, slot):
        return remote(
            out.at[c, slot], ret.at[mine, c], o_send.at[slot - 1, c], o_recv.at[slot - 1, c], same_core(slot)
        )

    def down_start(c):
        down[0, c] = averaged(2 * CHUNKS + c)
        to_pair(c).start()
        to_core(c).start()

    def down_relay(c):
        to_pair(c).wait_recv()
        pair_to_core(c).start()

    def down_finish(c):
        total = dot(hid[0].reshape(GROUP, HID), down[0, c])
        to_core(c).wait_recv()
        total += dot(hid_in[0].reshape(GROUP, HID), down[1, c])
        total += dot(hid_in[1].reshape(GROUP, HID), down[2, c])
        pair_to_core(c).wait_recv()
        total += dot(hid_in[2].reshape(GROUP, HID), down[3, c])
        out[c] = total.astype(jnp.bfloat16).reshape(4, ROWS, COLS)
        for slot in (3, 2, 1):
            give_back(c, slot).start()
        ret[mine, c] = out[c, 0]

    over(0, early_chunks, down_start)
    over(8, 12, lambda p: takes(p, rest))
    over(8, 12, lambda p: take_lane(p, range(8)))
    acc[...] = jnp.zeros_like(acc)

    def average_up(c, j):
        weight = averaged(2 * c + j)
        exchange(2 * c + j).wait_send()
        own[2 * c + j] = weight

    def forward_next(index):
        c, j = index // 2, index % 2
        average_up(c, j)

        def body(q):
            acc[j, q] += dot_last(group(2, q, c), own[index])

        over(0, 4, body)

    over(0, 2 * CHUNKS - 1, forward_next)
    over(0, early_chunks, down_relay)
    average_up(CHUNKS - 1, 1)

    def hidden(n):
        q, to = ((2, other_core(0)), (1, same_core(-1)), (3, other_core(-1)))[n]
        return remote(hid.at[q], hid_in.at[n], h_send.at[n], h_recv.at[n], to)

    def activate(q):
        gate = acc[0, q]
        up = acc[1, q] + dot_last(group(2, q, CHUNKS - 1), own[2 * CHUNKS - 1])
        value = (gate * jax.nn.sigmoid(gate) * up).astype(jnp.bfloat16)
        hid[q] = value.reshape(4, ROWS, HID)

    def activate_send(n):
        activate(3 - n)
        for when, copy in ((0, 2), (1, 0), (2, 1)):

            @pl.when(n == when)
            def _():
                hidden(copy).start()

    over(0, 4, activate_send)
    for n in range(3):
        hidden(n).wait_recv()

    def down_steps(c):
        if early_chunks == 3:

            @pl.when(c == 2)
            def _():
                down_start(3)

            @pl.when(c == 3)
            def _():
                down_relay(3)

        else:

            @pl.when(c >= 2)
            def _():
                down_start(c)
                down_relay(c)

        down_finish(c)

    over(0, CHUNKS, down_steps)

    next_gates = column(next_gates_ref[...])

    def mix(c, largest):
        for slot, hops in ((1, 1), (2, -2), (3, 3)):
            here = ret.at[expert_at(hops), c]
            remote(here, here, o_send.at[slot - 1, c], o_recv.at[slot - 1, c], other_core(0)).wait_recv()
        value = dot(table[...], ret[:, c].reshape(EXPERTS * ROWS, COLS)) * next_gates
        mixed[c] = value
        return jnp.maximum(largest, jnp.max(jnp.abs(value), axis=1, keepdims=True))

    largest = lax.fori_loop(0, CHUNKS, mix, jnp.zeros((TOK, 1), jnp.float32))
    inverse = 1.0 / (largest + epsilon)

    def code(c):
        codes_ref[:, columns(c)] = (mixed[c] * inverse).astype(jnp.bfloat16)

    over(0, CHUNKS, code)
    lane = lax.broadcasted_iota(jnp.int32, (TOK, TOK), 1)
    across = lax.broadcasted_iota(jnp.int32, (TOK, TOK), 0)
    scales_ref[...] = jnp.sum(jnp.where(lane == across, largest, 0.0), axis=0, keepdims=True)

    def rows_sent(p):
        for copy in direct(p) + [relay(p, slot) for slot in near] + [forward(p, slot) for slot in range(1, 8)]:
            copy.wait_send()

    def chunk_sent(c):
        exchange(2 * CHUNKS + c).wait_send()
        to_pair(c).wait_send()
        to_core(c).wait_send()
        pair_to_core(c).wait_send()
        for slot in near:
            give_back(c, slot).wait_send()

    over(0, KINDS * CHUNKS, rows_sent)
    for n in range(3):
        hidden(n).wait_send()
    over(0, CHUNKS, chunk_sent)


def step(level, routes, gates, next_routes, next_gates, tokens, cotangent, next_tokens, weights):
    vmem = pl.BlockSpec(memory_space=pltpu.VMEM)
    hbm = pl.BlockSpec(memory_space=pl.ANY)
    bf16, f32 = jnp.bfloat16, jnp.float32
    dma = pltpu.SemaphoreType.DMA
    return pl.pallas_call(
        functools.partial(kernel, level),
        out_shape=(
            jax.ShapeDtypeStruct((TOK, D), bf16),
            jax.ShapeDtypeStruct((1, TOK), f32),
        ),
        in_specs=[vmem] * 4 + [hbm] * 4,
        out_specs=(vmem, vmem),
        scratch_shapes=[
            pltpu.VMEM((3, TOK, D), bf16),
            pltpu.VMEM((3, HID, D), bf16),
            pltpu.VMEM((KINDS * CHUNKS, EXPERTS, ROWS, COLS), bf16),
            pltpu.VMEM((KINDS * CHUNKS, 4, 4, ROWS, COLS), bf16),
            pltpu.VMEM((4, HID, GROUP), f32),
            pltpu.VMEM((4, HID, GROUP), f32),
            pltpu.VMEM((4, HID, GROUP), f32),
            pltpu.VMEM((3, 4, HID, GROUP), bf16),
            pltpu.VMEM((3 * CHUNKS, HID, COLS), bf16),
            pltpu.VMEM((3 * CHUNKS, HID, COLS), bf16),
            pltpu.VMEM((2, 4, GROUP, HID), f32),
            pltpu.VMEM((4, 4, ROWS, HID), bf16),
            pltpu.VMEM((3, 4, ROWS, HID), bf16),
            pltpu.VMEM((4, CHUNKS, HID, COLS), bf16),
            pltpu.VMEM((CHUNKS, 4, ROWS, COLS), bf16),
            pltpu.VMEM((EXPERTS, CHUNKS, ROWS, COLS), bf16),
            pltpu.VMEM((CHUNKS, TOK, COLS), f32),
            pltpu.VMEM((TOK, EXPERTS * ROWS), bf16),
            dma((CHUNKS + 3,)),
            dma((KINDS * CHUNKS, 15)),
            dma((KINDS * CHUNKS, 16)),
            dma((3 * CHUNKS,)),
            dma((3 * CHUNKS,)),
            dma((3,)),
            dma((3,)),
            dma((3, CHUNKS)),
            dma((3, CHUNKS)),
            dma((3, CHUNKS)),
            dma((3, CHUNKS)),
        ],
        compiler_params=pltpu.CompilerParams(
            collective_id=level, has_side_effects=True, vmem_limit_bytes=48 * 2**20
        ),
        name=f"step_{level}",
    )(routes, gates, next_routes, next_gates, tokens, cotangent, next_tokens, weights)


def local(
    weights,
    tokens,
    cotangent,
    routes,
    gate_weights,
    next_tokens,
    next_routes,
    next_gates,
    step_index,
):
    branches = [functools.partial(step, level) for level in range(LEVELS)]
    codes, scales = lax.switch(
        step_index[0] % LEVELS,
        branches,
        routes.reshape(1, TOK),
        gate_weights.reshape(1, TOK),
        next_routes.reshape(1, TOK),
        next_gates.reshape(1, TOK),
        tokens[0],
        cotangent[0],
        next_tokens[0],
        weights[0],
    )
    return (codes[None], scales)


def solution(mesh):
    placed = (
        P("replica", None, "expert", None),
        P("replica", "expert", None),
        P("replica", "expert", None),
        P("replica", "expert", None),
        P("replica", "expert", None),
        P("replica", "expert", None),
        P("replica", "expert", None),
        P("replica", "expert", None),
        P(),
    )
    return jax.shard_map(
        local,
        mesh=mesh,
        in_specs=placed,
        out_specs=(P("replica", "expert", None), P("replica", "expert")),
        check_vma=False,
    )
```

profile of v0, /device:TPU:1, one launch (start us, length us, event | category | flops | bytes accessed | tf_op | source)
XLA Modules:
  0.0 131.4 jit_solution(4257021006934198247)
XLA Ops:
  1.3 128.8 %conditional.1 = (f32[1,128]{1,0:T(1,128)S(1)}, bf16[1,128,2048]{2,1,0:T(8,128)(2,1)S(1)}) conditional(s32[]{:T(128)} %clamp.3, (s32[1,128]{1,0:T(1,128)}, f32[1,128]{1,0:T(1,128)}, s32[1,128]{1,0:T(1,128)}, f32[1,128]{1,0:T(1,128)}, bf16[128,2048]{1,0:T(8,128)(2,1)}, /*index=5*/bf16[128,2048]{1,0:T(8,128)(2,1)}, ...), branch_computations={%region_0.1_spmd, %region_1.2_spmd, %region_2.3_spmd, %region_3.4_... | conditional | bytes 16 | solution.py:526
  1.3 128.5 %step_0.1 = (bf16[128,2048]{1,0:T(8,128)(2,1)S(1)}, f32[1,128]{1,0:T(1,128)S(1)}) custom-call(s32[1,128]{1,0:T(1,128)} %get-tuple-element.73.routes_ref, f32[1,128]{1,0:T(1,128)} %get-tuple-element.74.gates_ref, s32[1,128]{1,0:T(1,128)} %get-tuple-element.75.next_routes_ref, f32[1,128]{1,0:T(1,128)} %get-tuple-element.76.next_gates_ref, ...), custom_call_target="tpu_custom_call" | custom-call | tf_op jit(solution)/shard_map/cond/branch_0_fun/step_0/pallas_call | solution.py:468
  130.1 0.8 copy.22
  130.9 0.5 copy.23
where the time goes:
time: 132 us; the launch traced here: 131 us
  Pallas kernels  129 us (98%)
    pallas_call x1, Pallas kernels, step(): pl.pallas_call(functools.partial(kernel, level), out_shape=(jax.ShapeDtyp...  129 us

commit v1 on v0

--- a/solution.py
+++ b/solution.py
@@ -21,6 +21,9 @@
 GROUP = 4 * ROWS
 KINDS = 3
 EARLY = (3, 2, 2, 3)
+FINE = 256
+FINES = D // FINE
+SPLIT = COLS // FINE
 RATE = 2.0 / math.sqrt(D * 16 * CAP)
 epsilon = 1e-06
 MESH = pl.DeviceIdType.MESH
@@ -56,6 +59,10 @@
 
 def columns(c):
     return pl.ds(pl.multiple_of(c * COLS, COLS), COLS)
+
+
+def fine_columns(c):
+    return pl.ds(pl.multiple_of(c * FINE, FINE), FINE)
 
 
 def kernel(
@@ -74,12 +81,13 @@
     w_ref,
     block,
     rows,
-    gate_t,
-    up_t,
+    pre_t,
     back_t,
     d_t,
     own,
     theirs,
+    own_down,
+    their_down,
     acc,
     hid,
     hid_in,
@@ -93,6 +101,8 @@
     x_recv,
     g_send,
     g_recv,
+    f_send,
+    f_recv,
     h_send,
     h_recv,
     d_send,
@@ -227,26 +237,23 @@
         return rows[kind * CHUNKS + c, q].reshape(GROUP, COLS)
 
     def forward_x(q):
-        gate_t[q] = jnp.zeros((HID, GROUP), jnp.float32)
-        up_t[q] = jnp.zeros((HID, GROUP), jnp.float32)
+        pre_t[q] = jnp.zeros((2 * HID, GROUP), jnp.float32)
         back_t[q] = jnp.zeros((HID, GROUP), jnp.float32)
 
         def body(c):
-            value = group(0, q, c)
-            gate_t[q] += dot_last(w_ref[0, :, columns(c)], value)
-            up_t[q] += dot_last(w_ref[1, :, columns(c)], value)
+            pre_t[q] += dot_last(w_ref[0:2, :, columns(c)].reshape(2 * HID, COLS), group(0, q, c))
 
         over(0, CHUNKS, body)
-        gate = gate_t[q]
-        d_t[2, q] = (gate * jax.nn.sigmoid(gate) * up_t[q]).astype(jnp.bfloat16)
+        gate = pre_t[q, 0:HID]
+        d_t[2, q] = (gate * jax.nn.sigmoid(gate) * pre_t[q, HID:]).astype(jnp.bfloat16)
 
     def backward(q, c):
         back_t[q] += dot_last(w_ref[2, :, columns(c)], group(1, q, c))
 
     def slopes(q):
         back = back_t[q]
-        gate = gate_t[q]
-        up = up_t[q]
+        gate = pre_t[q, 0:HID]
+        up = pre_t[q, HID:]
         logistic = jax.nn.sigmoid(gate)
         d_t[0, q] = (back * up * (logistic * (1.0 + gate * (1.0 - logistic)))).astype(jnp.bfloat16)
         d_t[1, q] = (back * (gate * logistic)).astype(jnp.bfloat16)
@@ -254,14 +261,19 @@
     def exchange(index):
         return remote(own.at[index], theirs.at[index], g_send.at[index], g_recv.at[index], partner)
 
-    def update(j, c, index):
+    def exchange_down(c):
+        return remote(own_down.at[c], their_down.at[c], f_send.at[c], f_recv.at[c], partner)
+
+    def updated(j, c):
         cols = columns(c)
-        kind = j // 2
         grad = jnp.zeros((HID, COLS), jnp.float32)
         for q in range(4):
-            grad += dot(d_t[j, q], group(kind, q, c))
+            grad += dot(d_t[j, q], group(j // 2, q, c))
         grad = grad.astype(jnp.bfloat16).astype(jnp.float32)
-        own[index] = (w_ref[j, :, cols].astype(jnp.float32) - RATE * grad).astype(jnp.bfloat16)
+        return (w_ref[j, :, cols].astype(jnp.float32) - RATE * grad).astype(jnp.bfloat16)
+
+    def update(j, c, index):
+        own[index] = updated(j, c)
         exchange(index).start()
 
     def update_up(c):
@@ -269,7 +281,10 @@
         takes(8 + c, near)
 
     def update_down(c):
-        update(2, c, 2 * CHUNKS + c)
+        value = updated(2, c)
+        for n in range(SPLIT):
+            own_down[SPLIT * c + n] = value[:, n * FINE : (n + 1) * FINE]
+            exchange_down(SPLIT * c + n).start()
 
     near, rest = (1, 2, 3), (4, 5, 6, 7)
     over(0, 4, lambda p: takes(p, near))
@@ -301,16 +316,17 @@
         def _():
             takes(c + 6, near)
 
-    over(0, 3, early)
-    takes(7, rest)
-    over(8, 12, dispatch)
-    take_lane(7, range(8))
-
     def backward_last(q):
         backward(q, CHUNKS - 1)
         slopes(q)
 
-    over(0, 4, backward_last)
+    over(0, 3, early)
+    take_lane(7, (0, 1, 2, 3))
+    over(0, 2, lambda lane: backward_last(2 * lane))
+    takes(7, rest)
+    over(8, 12, dispatch)
+    take_lane(7, rest)
+    over(0, 2, lambda lane: backward_last(2 * lane + 1))
     over(0, CHUNKS, update_up)
     over(early_chunks, CHUNKS, update_down)
 
@@ -319,6 +335,11 @@
         both = own[index].astype(jnp.float32) + theirs[index].astype(jnp.float32)
         return (both * 0.5).astype(jnp.bfloat16)
 
+    def averaged_down(c):
+        exchange_down(c).wait_recv()
+        both = own_down[c].astype(jnp.float32) + their_down[c].astype(jnp.float32)
+        return (both * 0.5).astype(jnp.bfloat16)
+
     def to_core(c):
         return remote(down.at[0, c], down.at[1, c], d_send.at[0, c], d_recv.at[0, c], other_core(0))
 
@@ -334,7 +355,7 @@
         )
 
     def down_start(c):
-        down[0, c] = averaged(2 * CHUNKS + c)
+        down[0, c] = averaged_down(c)
         to_pair(c).start()
         to_core(c).start()
 
@@ -349,14 +370,13 @@
         total += dot(hid_in[1].reshape(GROUP, HID), down[2, c])
         pair_to_core(c).wait_recv()
         total += dot(hid_in[2].reshape(GROUP, HID), down[3, c])
-        out[c] = total.astype(jnp.bfloat16).reshape(4, ROWS, COLS)
+        out[c] = total.astype(jnp.bfloat16).reshape(4, ROWS, FINE)
         for slot in (3, 2, 1):
             give_back(c, slot).start()
         ret[mine, c] = out[c, 0]
 
-    over(0, early_chunks, down_start)
-    over(8, 12, lambda p: takes(p, rest))
-    over(8, 12, lambda p: take_lane(p, range(8)))
+    early_fines = SPLIT * early_chunks
+    over(0, early_fines, down_start)
     acc[...] = jnp.zeros_like(acc)
 
     def average_up(c, j):
@@ -366,6 +386,12 @@
 
     def forward_next(index):
         c, j = index // 2, index % 2
+
+        @pl.when(j == 0)
+        def _():
+            takes(8 + c, rest)
+            take_lane(8 + c, range(8))
+
         average_up(c, j)
 
         def body(q):
@@ -374,7 +400,6 @@
         over(0, 4, body)
 
     over(0, 2 * CHUNKS - 1, forward_next)
-    over(0, early_chunks, down_relay)
     average_up(CHUNKS - 1, 1)
 
     def hidden(n):
@@ -396,30 +421,23 @@
                 hidden(copy).start()
 
     over(0, 4, activate_send)
+    over(0, early_fines, down_relay)
+    down_start(early_fines)
     for n in range(3):
         hidden(n).wait_recv()
 
     def down_steps(c):
-        if early_chunks == 3:
-
-            @pl.when(c == 2)
-            def _():
-                down_start(3)
-
-            @pl.when(c == 3)
-            def _():
-                down_relay(3)
-
-        else:
-
-            @pl.when(c >= 2)
-            def _():
-                down_start(c)
-                down_relay(c)
+        @pl.when((c >= early_fines - 1) & (c < FINES - 2))
+        def _():
+            down_start(c + 2)
+
+        @pl.when(c >= early_fines)
+        def _():
+            down_relay(c)
 
         down_finish(c)
 
-    over(0, CHUNKS, down_steps)
+    over(0, FINES, down_steps)
 
     next_gates = column(next_gates_ref[...])
 
@@ -427,17 +445,17 @@
         for slot, hops in ((1, 1), (2, -2), (3, 3)):
             here = ret.at[expert_at(hops), c]
             remote(here, here, o_send.at[slot - 1, c], o_recv.at[slot - 1, c], other_core(0)).wait_recv()
-        value = dot(table[...], ret[:, c].reshape(EXPERTS * ROWS, COLS)) * next_gates
+        value = dot(table[...], ret[:, c].reshape(EXPERTS * ROWS, FINE)) * next_gates
         mixed[c] = value
         return jnp.maximum(largest, jnp.max(jnp.abs(value), axis=1, keepdims=True))
 
-    largest = lax.fori_loop(0, CHUNKS, mix, jnp.zeros((TOK, 1), jnp.float32))
+    largest = lax.fori_loop(0, FINES, mix, jnp.zeros((TOK, 1), jnp.float32))
     inverse = 1.0 / (largest + epsilon)
 
     def code(c):
-        codes_ref[:, columns(c)] = (mixed[c] * inverse).astype(jnp.bfloat16)
-
-    over(0, CHUNKS, code)
+        codes_ref[:, fine_columns(c)] = (mixed[c] * inverse).astype(jnp.bfloat16)
+
+    over(0, FINES, code)
     lane = lax.broadcasted_iota(jnp.int32, (TOK, TOK), 1)
     across = lax.broadcasted_iota(jnp.int32, (TOK, TOK), 0)
     scales_ref[...] = jnp.sum(jnp.where(lane == across, largest, 0.0), axis=0, keepdims=True)
@@ -447,7 +465,7 @@
             copy.wait_send()
 
     def chunk_sent(c):
-        exchange(2 * CHUNKS + c).wait_send()
+        exchange_down(c).wait_send()
         to_pair(c).wait_send()
         to_core(c).wait_send()
         pair_to_core(c).wait_send()
@@ -457,7 +475,7 @@
     over(0, KINDS * CHUNKS, rows_sent)
     for n in range(3):
         hidden(n).wait_send()
-    over(0, CHUNKS, chunk_sent)
+    over(0, FINES, chunk_sent)
 
 
 def step(level, routes, gates, next_routes, next_gates, tokens, cotangent, next_tokens, weights):
@@ -478,31 +496,34 @@
             pltpu.VMEM((3, HID, D), bf16),
             pltpu.VMEM((KINDS * CHUNKS, EXPERTS, ROWS, COLS), bf16),
             pltpu.VMEM((KINDS * CHUNKS, 4, 4, ROWS, COLS), bf16),
-            pltpu.VMEM((4, HID, GROUP), f32),
-            pltpu.VMEM((4, HID, GROUP), f32),
+            pltpu.VMEM((4, 2 * HID, GROUP), f32),
             pltpu.VMEM((4, HID, GROUP), f32),
             pltpu.VMEM((3, 4, HID, GROUP), bf16),
-            pltpu.VMEM((3 * CHUNKS, HID, COLS), bf16),
-            pltpu.VMEM((3 * CHUNKS, HID, COLS), bf16),
+            pltpu.VMEM((2 * CHUNKS, HID, COLS), bf16),
+            pltpu.VMEM((2 * CHUNKS, HID, COLS), bf16),
+            pltpu.VMEM((FINES, HID, FINE), bf16),
+            pltpu.VMEM((FINES, HID, FINE), bf16),
             pltpu.VMEM((2, 4, GROUP, HID), f32),
             pltpu.VMEM((4, 4, ROWS, HID), bf16),
             pltpu.VMEM((3, 4, ROWS, HID), bf16),
-            pltpu.VMEM((4, CHUNKS, HID, COLS), bf16),
-            pltpu.VMEM((CHUNKS, 4, ROWS, COLS), bf16),
-            pltpu.VMEM((EXPERTS, CHUNKS, ROWS, COLS), bf16),
-            pltpu.VMEM((CHUNKS, TOK, COLS), f32),
+            pltpu.VMEM((4, FINES, HID, FINE), bf16),
+            pltpu.VMEM((FINES, 4, ROWS, FINE), bf16),
+            pltpu.VMEM((EXPERTS, FINES, ROWS, FINE), bf16),
+            pltpu.VMEM((FINES, TOK, FINE), f32),
             pltpu.VMEM((TOK, EXPERTS * ROWS), bf16),
             dma((CHUNKS + 3,)),
             dma((KINDS * CHUNKS, 15)),
             dma((KINDS * CHUNKS, 16)),
-            dma((3 * CHUNKS,)),
-            dma((3 * CHUNKS,)),
+            dma((2 * CHUNKS,)),
+            dma((2 * CHUNKS,)),
+            dma((FINES,)),
+            dma((FINES,)),
             dma((3,)),
             dma((3,)),
-            dma((3, CHUNKS)),
-            dma((3, CHUNKS)),
-            dma((3, CHUNKS)),
-            dma((3, CHUNKS)),
+            dma((3, FINES)),
+            dma((3, FINES)),
+            dma((3, FINES)),
+            dma((3, FINES)),
         ],
         compiler_params=pltpu.CompilerParams(
             collective_id=level, has_side_effects=True, vmem_limit_bytes=48 * 2**20

time: 132 us -> 131 us (level)
  Pallas kernels: 129 us -> 127 us
    pallas_call x1, Pallas kernels: 129 us -> 127 us  [step(): pl.pallas_call(functools.partial(kernel, level), out_shape=(jax.ShapeDtyp...]
where the time goes in v1:
time: 131 us; the launch traced here: 130 us
  Pallas kernels  127 us (97%)
  local copies, waits for them, and re-layouts  1.31 us (1%)
    pallas_call x1, Pallas kernels, step(): pl.pallas_call(functools.partial(kernel, level), out_shape=(jax.ShapeDtyp...  127 us

profile of v1, /device:TPU:1, one launch (start us, length us, event | category | flops | bytes accessed | tf_op | source)
XLA Modules:
  0.0 129.9 jit_solution(10871227894054206849)
XLA Ops:
  1.3 127.3 %conditional.1 = (f32[1,128]{1,0:T(1,128)S(1)}, bf16[1,128,2048]{2,1,0:T(8,128)(2,1)S(1)}) conditional(s32[]{:T(128)} %clamp.3, (s32[1,128]{1,0:T(1,128)}, f32[1,128]{1,0:T(1,128)}, s32[1,128]{1,0:T(1,128)}, f32[1,128]{1,0:T(1,128)}, bf16[128,2048]{1,0:T(8,128)(2,1)}, /*index=5*/bf16[128,2048]{1,0:T(8,128)(2,1)}, ...), branch_computations={%region_0.1_spmd, %region_1.2_spmd, %region_2.3_spmd, %region_3.4_... | conditional | bytes 16 | solution.py:547
  1.5 126.9 %step_3.1 = (bf16[128,2048]{1,0:T(8,128)(2,1)S(1)}, f32[1,128]{1,0:T(1,128)S(1)}) custom-call(s32[1,128]{1,0:T(1,128)} %get-tuple-element.103.routes_ref, f32[1,128]{1,0:T(1,128)} %get-tuple-element.104.gates_ref, s32[1,128]{1,0:T(1,128)} %get-tuple-element.105.next_routes_ref, f32[1,128]{1,0:T(1,128)} %get-tuple-element.106.next_gates_ref, ...), custom_call_target="tpu_custom_call" | custom-call | tf_op jit(solution)/shard_map/cond/branch_3_fun/step_3/pallas_call | solution.py:486
  128.6 0.8 copy.22
  129.4 0.5 copy.23
